TPU v7x, 32 devices: a whole 2x2x4 slice. The times are simulated.
32 devices in a mesh: chan: 16 (over z, y, x), tm: 2 (over core).
Axes of the slice: x: 2, y: 2, z: 4, core: 2. Of those that a mesh axis runs over, the one named last changes fastest.
Arguments:
- spectra: bfloat16 [2, 16, 10240, 2, 384], P('tm', 'chan'), as said below
- mask: int32 [2, 16, 10240], P('tm', 'chan'), may hold values from 0 to 1, as said below
Outputs:
- correlations: float32 [8, 10240, 3001], P('tm', 'chan')
Inputs may be any that keep to these rules, and one draw needn't show every extreme that they name: `spectra`: spectra of the windows, of scales that vary over bins and over channels. `mask`: in every window, among the 640 channels of one block (channels b * 640 to (b + 1) * 640 - 1) at most 480 flags are 1.
All inputs are finite; a program needn't handle non-finite values.
Results may differ from a plain program's by a relative error of at most 0.004.
Values may be sent and summed in bfloat16 or wider, within the bound.
A program may use at most 320 MiB of HBM per device.

v0:
```python
import math

import jax
import jax.numpy as jnp
from jax import lax
from jax.sharding import PartitionSpec as P

CH = 10240
F = 384
F0 = 12
NFFT = 6000
MAXLAG = 1500
SB = 4
STEPS = 2
LAGS = 3001


def spread(x, axis, root):
    mine = lax.axis_index(axis) == root
    return lax.psum(jnp.where(mine, x, jnp.zeros_like(x)), axis)


def lag_table():
    bin_index = F0 + jnp.arange(F, dtype=jnp.int32)
    lag_index = jnp.arange(LAGS, dtype=jnp.int32) - MAXLAG
    phase_steps = jnp.mod(bin_index[:, None] * lag_index[None, :], NFFT)
    angles = phase_steps.astype(jnp.float32) * jnp.float32(2.0 * math.pi / NFFT)
    return jnp.concatenate([jnp.cos(angles), -jnp.sin(angles)], axis=0)


def whiten(window_spec, kept_mask):
    values = window_spec.astype(jnp.float32)
    energy = jnp.sum(values * values, axis=(-2, -1)) / F
    factor = lax.rsqrt(energy + 1e-06) * kept_mask.astype(jnp.float32)
    return (values * factor[..., None, None]).astype(jnp.bfloat16)


def to_lags(cross_sum, block_width, lag_matrix):
    sources = cross_sum.shape[0]
    flat_cross = cross_sum.reshape(sources * block_width, 2 * F)
    lagged = jnp.dot(
        flat_cross, lag_matrix, precision=lax.Precision.HIGHEST, preferred_element_type=jnp.float32
    )
    return lagged.reshape(sources, block_width, LAGS)


def local(spectra, mask):
    blocks = lax.axis_size("chan")
    block_width = CH // blocks
    win_local = spectra.shape[1]
    whitened = whiten(spectra[0], mask[0])
    by_owner = whitened.reshape(win_local, blocks, block_width, 2, F)
    owner_mask = mask[0].reshape(win_local, blocks, block_width)
    got_rows, got_flags = (
        lax.all_to_all(by_owner, "chan", split_axis=1, concat_axis=0, tiled=True),
        lax.all_to_all(owner_mask, "chan", split_axis=1, concat_axis=0, tiled=True),
    )
    received = got_rows[:, 0]
    receiver_keep = got_flags[:, 0].astype(jnp.float32)
    stride = blocks // STEPS
    row_pieces = []
    keep_pieces = []
    for block in range(STEPS):
        got_block, got_keep = (
            spread(received[:, :SB], "chan", block * stride),
            spread(receiver_keep[:, :SB].astype(jnp.bfloat16), "chan", block * stride),
        )
        row_pieces.append(got_block)
        keep_pieces.append(got_keep)
    source_rows = jnp.concatenate(row_pieces, axis=1)
    source_keep = jnp.concatenate(keep_pieces, axis=1)
    products = jnp.einsum(
        "wqaj,wcbj->qcabj", source_rows, received, preferred_element_type=jnp.float32
    )
    real_part = products[:, :, 0, 0] + products[:, :, 1, 1]
    imag_part = products[:, :, 1, 0] - products[:, :, 0, 1]
    cross_sum = jnp.stack([real_part, imag_part], axis=2)
    pair_count = jnp.einsum("wq,wc->qc", source_keep.astype(jnp.float32), receiver_keep)
    lag_matrix = lag_table()
    lagged_all = to_lags(cross_sum, block_width, lag_matrix)
    lagged, count_part = (
        lax.psum_scatter(lagged_all, "tm", scatter_dimension=0, tiled=True),
        lax.psum_scatter(pair_count, "tm", scatter_dimension=0, tiled=True),
    )
    return lagged / jnp.maximum(count_part, 1.0)[:, :, None]


def solution(mesh):
    placed = (P("tm", "chan", None, None, None), P("tm", "chan", None))
    return jax.shard_map(
        local, mesh=mesh, in_specs=placed, out_specs=P("tm", "chan", None), check_vma=False
    )
```

profile of v0, /device:TPU:15, one launch (start us, length us, event | category | flops | bytes accessed | tf_op | source)
XLA Modules:
  0.0 1048.2 jit_solution(694322813584980071)
XLA Ops:
  6.5 0.0 copy-start
  6.5 18.4 %copy_convert_fusion = f32[1,1,10240,2,384]{4,2,3,1,0:T(8,128)} fusion(bf16[1,1,10240,2,384]{4,3,2,1,0:T(2,128)(2,1)} %param.2), kind=kLoop, calls=%fused_computation.5 | loop fusion | flops 7864320 | bytes 47185920 | tf_op jit(solution)/shard_map/convert_element_type | solution.py:32
  25.0 3.1 copy-done
  28.1 3.8 multiply_reduce_fusion
  31.9 0.9 convert_reduce_fusion
  32.8 11.8 %multiply_convert_fusion = bf16[1,16,640,2,384]{4,2,1,3,0:T(8,128)(2,1)S(1)} fusion(f32[1,16,640,2,384]{4,2,1,3,0:T(8,128)} %bitcast.43, f32[16,640]{1,0:T(8,128)S(1)} %mul.66), kind=kLoop, calls=%fused_computation | loop fusion | flops 15728640 | bytes 47226880 | tf_op jit(solution)/shard_map/convert_element_type | solution.py:35
  44.7 6.5 copy.28
  51.2 6.6 all-to-all-start
  57.8 0.0 all-reduce.5.cloned.1.call-start
  57.9 351.4 %all-to-all-done = bf16[1,16,640,2,384]{4,2,3,0,1:T(8,128)(2,1)} async-done(((bf16[1,16,640,2,384]{4,2,3,0,1:T(8,128)(2,1)}), bf16[1,16,640,2,384]{4,2,3,0,1:T(8,128)(2,1)}, u32[]{:S(2)}, u32[]{:S(2)}) %all-to-all-start) | async-done | bytes 15728672 | tf_op jit(solution)/shard_map/all_to_all | solution.py:55
  409.3 100.5 %copy.29 = bf16[1,16,640,2,384]{1,2,3,4,0:T(8,128)(2,1)} copy(bf16[1,16,640,2,384]{4,2,3,0,1:T(8,128)(2,1)} %all-to-all-done) | data formatting | bytes 31457280 | tf_op jit(solution)/shard_map/all_to_all | solution.py:55
  509.8 3.0 broadcast_select_fusion.1
  512.8 0.0 all-reduce.5.cloned.1.call-update
  512.8 0.0 reduce-scatter.2.cloned.1.call-start
  512.9 20.7 %fusion.11 = (f32[384,3001]{0,1:T(8,128)}, f32[384,3001]{0,1:T(8,128)}) fusion(s32[3001]{0:T(1024)S(1)} %iota_add_fusion, s32[384]{0:T(512)S(1)} %iota_add_fusion.1), kind=kLoop, calls=%fused_computation.24 | loop fusion | flops 11523840 | bytes 9232612 | tf_op jit(solution)/shard_map/cos | solution.py:28
  533.6 100.5 %copy.35 = bf16[16,640,2,384,1]{0,1,4,2,3:T(8,128)(2,1)} copy(bf16[16,640,2,384,1]{3,1,2,0,4:T(8,128)(2,1)} %bitcast.3) | data formatting | bytes 31457280 | tf_op jit(solution)/shard_map/squeeze | solution.py:58
  634.1 3.2 all-reduce.5.cloned.1.call-done
  637.3 55.3 %convolution_bitcast_fusion = f32[8,640,2,2,384]{1,0,2,3,4:T(8,128)} fusion(bf16[16,640,2,384,1]{0,1,4,2,3:T(8,128)(2,1)} %copy.35, bf16[16,4,2,384]{0,1,2,3:T(4,128)(2,1)} %get-tuple-element.7, bf16[16,4,2,384]{0,1,2,3:T(4,128)(2,1)} %get-tuple-element.8), kind=kOutput, calls=%fused_computation.7 | convolution fusion | flops 252051456 | bytes 47382528 | tf_op jit(solution)/shard_map/wqaj,wcbj->qcabj/dot_general | solution.py:72
  692.6 9.3 fusion.4
  701.9 9.5 fusion.6
  711.4 12.3 %pad_maximum_fusion = f32[8,640,2,384]{1,0,3,2:T(8,128)} fusion(f32[8,640,1,384]{1,0,3,2:T(8,128)} %fusion.4, f32[8,640,1,384]{1,0,3,2:T(8,128)} %fusion.6), kind=kLoop, calls=%fused_computation.2 | loop fusion | flops 3932160 | bytes 31457280 | tf_op jit(solution)/shard_map/stack | solution.py:77
  723.7 160.3 %fusion = f32[8,640,3001]{1,2,0:T(8,128)} fusion(f32[8,640,768]{1,0,2:T(8,128)} %bitcast.44, f32[384,3001]{0,1:T(8,128)} %get-tuple-element.14, f32[384,3001]{0,1:T(8,128)} %get-tuple-element.13), kind=kOutput, calls=%fused_computation.3 | convolution fusion | flops 141607256064 | bytes 86408192 | tf_op jit(solution)/shard_map/dot_general | solution.py:41
  884.0 0.0 copy-start.1
  884.0 0.0 reduce-scatter.2.cloned.1.call-update
  884.0 8.4 all-to-all-start.1
  892.4 0.0 copy-done.1
  892.4 0.6 dynamic-slice
  893.6 2.4 all-to-all-done.1
  896.1 24.0 %all-reduce.1 = (bf16[16,4]{1,0:T(8,128)(2,1)S(1)}, bf16[16,4]{1,0:T(8,128)(2,1)S(1)}) all-reduce(bf16[16,4]{1,0:T(8,128)(2,1)S(1)} %get-tuple-element.12, bf16[16,4]{1,0:T(8,128)(2,1)S(1)} %get-tuple-element.11), channel_id=1, replica_groups=mesh['chan'=16,'tm'=2] {'chan'}, use_global_device_ids=true, to_apply=%region_5.6 | all-reduce | flops 128 | bytes 512 | tf_op jit(solution)/shard_map/psum | solution.py:20
  920.1 0.3 fusion.15
  920.3 13.0 %all-reduce = f32[8,640]{1,0:T(8,128)S(1)} all-reduce(f32[8,640]{1,0:T(8,128)S(1)} %fusion.15), channel_id=3, replica_groups=mesh['chan'=16,'tm'=2] {'tm'}, use_global_device_ids=true, to_apply=%region_6.7.clone | all-reduce | flops 5120 | bytes 40960
  933.3 31.8 %reduce-scatter.2.cloned.1.call-done = f32[4,640,3001]{1,2,0:T(8,128)} async-done(((f32[8,640,3001]{1,2,0:T(8,128)}), f32[4,640,3001]{1,2,0:T(8,128)}) %reduce-scatter.2.cloned.1.call-update) | async-done | bytes 30730256 | tf_op jit(solution)/shard_map/reduce_scatter | solution.py:82
  965.1 21.3 %broadcast_divide_fusion = f32[4,640,3001]{1,2,0:T(8,128)} fusion(f32[4,640,3001]{1,2,0:T(8,128)} %reduce-scatter.2.cloned.1.call-done, f32[4,640]{1,0:T(4,128)S(1)} %dynamic-slice_maximum_fusion), kind=kLoop, calls=%fused_computation.6 | loop fusion | flops 7682560 | bytes 61470720 | tf_op jit(solution)/shard_map/div | solution.py:85
  986.4 54.9 %copy.34 = f32[4,640,3001]{1,0,2:T(4,128)} copy(f32[4,640,3001]{1,2,0:T(8,128)} %broadcast_divide_fusion) | data formatting | bytes 61460480 | tf_op jit(solution)/shard_map/div | solution.py:85
  (10 shorter events, 0.1 us)
Async XLA Ops:
  6.5 21.6 %copy-start = (bf16[1,1,10240,2,384]{4,3,2,1,0:T(2,128)(2,1)S(1)}, bf16[1,1,10240,2,384]{4,3,2,1,0:T(2,128)(2,1)}, u32[]{:S(2)}) copy-start(bf16[1,1,10240,2,384]{4,3,2,1,0:T(2,128)(2,1)} %param.2) | copy-start | bytes 47185924
  51.2 358.1 %all-to-all-start = ((bf16[1,16,640,2,384]{4,2,3,0,1:T(8,128)(2,1)}), bf16[1,16,640,2,384]{4,2,3,0,1:T(8,128)(2,1)}, u32[]{:S(2)}, u32[]{:S(2)}) async-start(bf16[1,16,640,2,384]{4,2,3,0,1:T(8,128)(2,1)} %copy.28), calls=%async_computation | async-start | bytes 31457280 | tf_op jit(solution)/shard_map/all_to_all | solution.py:55
  57.8 579.5 %all-reduce.5.cloned.1.call-start = ((), (), s32[]{:S(2)}) async-start(), calls=%async_computation.4 | async-start | bytes 3145728 | tf_op jit(solution)/shard_map/psum | solution.py:20
  512.8 452.3 %reduce-scatter.2.cloned.1.call-start = ((), (), s32[]{:S(2)}) async-start(), calls=%async_computation.3 | async-start | bytes 92405760 | tf_op jit(solution)/shard_map/reduce_scatter | solution.py:82
  884.0 8.4 copy-start.1
  884.0 12.0 %all-to-all-start.1 = ((s32[1,16,640]{2,0,1:T(1,128)}), s32[1,16,640]{2,0,1:T(1,128)S(1)}, u32[]{:S(2)}, u32[]{:S(2)}) async-start(s32[1,16,640]{2,0,1:T(1,128)} %bitcast.11), calls=%async_computation.2 | async-start | bytes 81920 | tf_op jit(solution)/shard_map/all_to_all | solution.py:56
Sparse Core Ops, SparseCore 0:
  513.0 124.3 all-reduce.4
  884.2 80.9 reduce-scatter.1
where the time goes:
time: 1050 us
  waiting for transfers between devices  389 us (37%)
  local copies, waits for them, and re-layouts  266 us (25%)
  matrix products  216 us (21%)
  other arithmetic  111 us (11%)
  blocking collectives  36.9 us (4%)
  starting transfers between devices  15 us (1%)
  between operations  14.2 us (1%)
    all_to_all x1, waiting for transfers between devices, local(): lax.all_to_all(by_owner, 'chan', split_axis=1, concat_axis=0, tiled=True)  351 us
    dot_general x1, matrix products, to_lags(): jnp.dot(flat_cross, lag_matrix, precision=lax.Precision.HIGHEST, preferre...  160 us
    squeeze x1, local copies, waits for them, and re-layouts, local(): received = got_rows[:, 0]  100 us
    all_to_all x1, local copies, waits for them, and re-layouts, local(): lax.all_to_all(by_owner, 'chan', split_axis=1, concat_axis=0, tiled=True)  100 us
    dot_general x1, matrix products, local(): jnp.einsum('wqaj,wcbj->qcabj', source_rows, received, preferred_element_t...  55.3 us
    div x1, local copies, waits for them, and re-layouts, local(): return lagged / jnp.maximum(count_part, 1.0)[:, :, None]  54.9 us
    reduce_scatter x1, waiting for transfers between devices, local(): lax.psum_scatter(lagged_all, 'tm', scatter_dimension=0, tiled=True)  31.8 us
    psum x1, blocking collectives, spread(): return lax.psum(jnp.where(mine, x, jnp.zeros_like(x)), axis)  24 us
  transfers between devices with their start and end apart: 4, of which 4 were waited for; matrix products, arithmetic and copies ran while one was open for 12% of the time, Pallas kernels for 0%

commit v1 on v0

v1 whole, which is shorter than its diff:
```python
import functools
import math

import jax
import jax.numpy as jnp
import numpy as np
from jax import lax
from jax.experimental import pallas as pl
from jax.experimental.pallas import tpu as pltpu
from jax.sharding import PartitionSpec as P

CH = 10240
F = 384
F0 = 12
NFFT = 6000
MAXLAG = 1500
SB = 4
STEPS = 2
SRC = SB * STEPS
LAGS = 3001
LANES = 128
TILE = 128
MESH = pl.DeviceIdType.MESH


def lag_table():
    bins = F0 + np.arange(F, dtype=np.int64)
    lags = np.arange(LAGS, dtype=np.int64) - MAXLAG
    angles = np.mod(lags[:, None] * bins[None, :], NFFT) * (2.0 * math.pi / NFFT)
    table = np.concatenate([np.cos(angles), -np.sin(angles)], axis=1)
    return jnp.asarray(table.astype(np.float32)).astype(jnp.bfloat16)


def whiten(values):
    energy = jnp.sum(values * values, axis=(-2, -1), keepdims=True) / F
    return values * lax.rsqrt(energy + 1e-06)


def offset(step, n):
    return n // 2 + (1 - 2 * (step % 2)) * ((step + 1) // 2)


def exchange_kernel(
    n, bw, capp, x_ref, aux_ref, src_ref, out_ref,
    xin, pk, rv, fw, aux_rv, aux_fw, acc, cnt,
    in_sem, send_sem, recv_sem, asend_sem, arecv_sem,
    fsend_sem, frecv_sem, afsend_sem, afrecv_sem,
):
    me = lax.axis_index("chan")
    tm = lax.axis_index("tm")
    other = 1 - tm
    chunks = -(-bw // LANES)

    barrier = pltpu.get_barrier_semaphore()

    def greet(k, _):
        pl.semaphore_signal(barrier, inc=1, device_id=((me + k) % n, tm), device_id_type=MESH)
        return 0

    lax.fori_loop(1, n, greet, 0)
    pl.semaphore_signal(barrier, inc=1, device_id=(me, other), device_id_type=MESH)
    pl.semaphore_wait(barrier, n)

    def dest(step):
        return (me + offset(step, n)) % n

    def load(step):
        rows = pl.ds(pl.multiple_of(dest(step) * bw, bw), bw)
        return pltpu.make_async_copy(
            x_ref.at[:, rows, :], xin.at[step % 2], in_sem.at[step % 2]
        )

    def pack(step):
        load(step).wait()
        slot = step % 2
        re = xin[slot, 0].astype(jnp.float32)
        im = xin[slot, 1].astype(jnp.float32)
        energy = jnp.sum(re * re + im * im, axis=1, keepdims=True) / F
        factor = lax.rsqrt(energy + 1e-06)
        re = (re * factor).astype(jnp.bfloat16)
        im = (im * factor).astype(jnp.bfloat16)
        place = lax.broadcasted_iota(jnp.int32, (capp, LANES), 0).astype(jnp.float32)
        pick = jnp.concatenate(
            [
                jnp.where(place == aux_ref[dest(step), i : i + 1, :], 1.0, 0.0).astype(jnp.bfloat16)
                for i in range(chunks)
            ],
            axis=1,
        )[:, :bw]
        pk[step, 0:capp, :] = jnp.dot(pick, re, preferred_element_type=jnp.float32).astype(jnp.bfloat16)
        pk[step, capp : 2 * capp, :] = jnp.dot(pick, im, preferred_element_type=jnp.float32).astype(jnp.bfloat16)
        pk[step, 2 * capp :, :] = src_ref[...]

    def main(step):
        to = (dest(step), tm)
        return (
            pltpu.make_async_remote_copy(
                src_ref=pk.at[step], dst_ref=rv.at[step], send_sem=send_sem.at[step],
                recv_sem=recv_sem.at[step], device_id=to, device_id_type=MESH,
            ),
            pltpu.make_async_remote_copy(
                src_ref=aux_ref.at[dest(step)], dst_ref=aux_rv.at[step], send_sem=asend_sem.at[step],
                recv_sem=arecv_sem.at[step], device_id=to, device_id_type=MESH,
            ),
        )

    def forward(step, rows, flags):
        to = (me, other)
        return (
            pltpu.make_async_remote_copy(
                src_ref=rows, dst_ref=fw.at[step], send_sem=fsend_sem.at[step],
                recv_sem=frecv_sem.at[step], device_id=to, device_id_type=MESH,
            ),
            pltpu.make_async_remote_copy(
                src_ref=flags, dst_ref=aux_fw.at[step], send_sem=afsend_sem.at[step],
                recv_sem=afrecv_sem.at[step], device_id=to, device_id_type=MESH,
            ),
        )

    load(0).start()

    def send(step, _):
        load(step + 1).start()
        pack(step)
        for copy in main(step):
            copy.start()
        return 0

    lax.fori_loop(0, n - 1, send, 0)
    last = n - 1
    pack(last)
    for copy in forward(last, pk.at[last], aux_ref.at[me]):
        copy.start()

    acc[...] = jnp.zeros_like(acc)
    cnt[...] = jnp.zeros_like(cnt)
    late = tm.astype(jnp.float32)

    def correlate(rows, flags):
        sources = rows[2 * capp :, :].astype(jnp.float32)
        a_re = sources[0:SB] * (1.0 - late) + sources[SB : 2 * SB] * late
        a_im = sources[2 * SB : 3 * SB] * (1.0 - late) + sources[3 * SB :] * late
        source_keep = flags[chunks : chunks + 1, :]
        diagonal = lax.broadcasted_iota(jnp.int32, (LANES, LANES), 0) == lax.broadcasted_iota(
            jnp.int32, (LANES, LANES), 1
        )
        place = lax.broadcasted_iota(jnp.int32, (LANES, capp), 1).astype(jnp.float32)
        for i in range(chunks):
            here = slice(i * LANES, (i + 1) * LANES)
            rank = jnp.sum(jnp.where(diagonal, flags[i : i + 1, :], 0.0), axis=1, keepdims=True)
            back = jnp.where(place == rank, 1.0, 0.0).astype(jnp.bfloat16)
            b_re = jnp.dot(back, rows[0:capp, :], preferred_element_type=jnp.float32)
            b_im = jnp.dot(back, rows[capp : 2 * capp, :], preferred_element_type=jnp.float32)
            for q in range(SB):
                acc[q, here, 0:F] += a_re[q : q + 1] * b_re + a_im[q : q + 1] * b_im
                acc[q, here, F : 2 * F] += a_im[q : q + 1] * b_re - a_re[q : q + 1] * b_im
            cnt[here, :] += jnp.where(rank >= 0.0, 1.0, 0.0) * source_keep

    correlate(pk.at[last], aux_ref.at[me])

    def wait_forward(step):
        for copy in forward(step, rv.at[step], aux_rv.at[step]):
            copy.wait_recv()
        correlate(fw.at[step], aux_fw.at[step])

    wait_forward(last)

    def receive(step, _):
        for copy in main(step):
            copy.wait_recv()
        for copy in forward(step, rv.at[step], aux_rv.at[step]):
            copy.start()
        correlate(rv.at[step], aux_rv.at[step])
        wait_forward(step)
        return 0

    lax.fori_loop(0, n - 1, receive, 0)

    lane = lax.broadcasted_iota(jnp.int32, (1, LANES), 1)
    for q in range(SB):
        mine = jnp.where(lane == tm * SB + q, 1.0, 0.0)
        counted = jnp.sum(cnt[...] * mine, axis=1, keepdims=True)
        out_ref[q] = (acc[q] * (1.0 / jnp.maximum(counted, 1.0))).astype(out_ref.dtype)

    def finish(step, _):
        for copy in main(step):
            copy.wait_send()
        for copy in forward(step, rv.at[step], aux_rv.at[step]):
            copy.wait_send()
        return 0

    lax.fori_loop(0, n - 1, finish, 0)
    for copy in forward(last, pk.at[last], aux_ref.at[me]):
        copy.wait_send()


def exchange(x, aux, src, n, bw, capp):
    chunks = -(-bw // LANES)
    bwp = chunks * LANES
    rows = 2 * capp + 2 * SRC
    block = pltpu.VMEM((n, rows, F), jnp.bfloat16)
    flags = pltpu.VMEM((n, 8, LANES), jnp.float32)
    sems = pltpu.SemaphoreType.DMA((n,))
    return pl.pallas_call(
        functools.partial(exchange_kernel, n, bw, capp),
        out_shape=jax.ShapeDtypeStruct((SB, bwp, 2 * F), jnp.bfloat16),
        in_specs=[
            pl.BlockSpec(memory_space=pl.ANY),
            pl.BlockSpec(memory_space=pltpu.VMEM),
            pl.BlockSpec(memory_space=pltpu.VMEM),
        ],
        out_specs=pl.BlockSpec(memory_space=pltpu.VMEM),
        scratch_shapes=[
            pltpu.VMEM((2, 2, bw, F), jnp.bfloat16),
            block, block, block, flags, flags,
            pltpu.VMEM((SB, bwp, 2 * F), jnp.float32),
            pltpu.VMEM((bwp, LANES), jnp.float32),
            pltpu.SemaphoreType.DMA((2,)),
        ] + [sems] * 8,
        compiler_params=pltpu.CompilerParams(
            collective_id=0, has_side_effects=True, vmem_limit_bytes=62 * 1024 * 1024
        ),
        name="exchange_correlate",
    )(x, aux, src)


def lags_kernel(bw, table_ref, cross_ref, out_ref, mixed):
    for q in range(SB):
        lagged = lax.dot_general(
            table_ref[...], cross_ref[q], (((1,), (1,)), ((), ())), preferred_element_type=jnp.float32
        )
        for i in range(mixed.shape[0]):
            mixed[i, pl.ds(q, TILE, stride=SB), :] = lagged[:, i * LANES : (i + 1) * LANES]
    for i in range(mixed.shape[0]):
        width = min(bw - i * LANES, LANES)
        block = mixed[i].reshape(TILE, SB, LANES)
        out_ref[:, :, i * LANES : i * LANES + width] = block[:, :, :width]


def to_lags(cross, table, bw):
    chunks = cross.shape[1] // LANES
    out = pl.pallas_call(
        functools.partial(lags_kernel, bw),
        grid=(-(-LAGS // TILE),),
        out_shape=jax.ShapeDtypeStruct((LAGS, SB, bw), jnp.float32),
        in_specs=[
            pl.BlockSpec((TILE, 2 * F), lambda t: (t, 0)),
            pl.BlockSpec((SB, chunks * LANES, 2 * F), lambda t: (0, 0, 0)),
        ],
        out_specs=pl.BlockSpec((TILE, SB, bw), lambda t: (t, 0, 0)),
        scratch_shapes=[pltpu.VMEM((chunks, TILE * SB, LANES), jnp.float32)],
        compiler_params=pltpu.CompilerParams(vmem_limit_bytes=48 * 1024 * 1024),
        name="to_lags",
    )(table, cross)
    return out.transpose(1, 2, 0)


def local(table, spectra, mask):
    n = lax.axis_size("chan")
    bw = CH // n
    cap = bw * 3 // 4
    capp = -(-cap // 16) * 16
    chunks = -(-bw // LANES)
    x = spectra[0, 0].transpose(1, 0, 2)
    keep = mask[0, 0].reshape(n, bw)
    upto = jnp.arange(bw)[:, None] <= jnp.arange(bw)[None, :]
    count = jnp.dot(
        keep.astype(jnp.bfloat16), upto.astype(jnp.bfloat16), preferred_element_type=jnp.float32
    )
    rank = jnp.where(keep > 0, count - 1.0, -1.0)
    rank = jnp.pad(rank, ((0, 0), (0, chunks * LANES - bw)), constant_values=-1.0)
    stride = n // STEPS
    source_keep = keep[::stride, :SB].reshape(1, 1, SRC).astype(jnp.float32)
    source_keep = jnp.broadcast_to(jnp.pad(source_keep, ((0, 0), (0, 0), (0, LANES - SRC))), (n, 1, LANES))
    aux = jnp.concatenate([rank.reshape(n, chunks, LANES), source_keep], axis=1)
    aux = jnp.pad(aux, ((0, 0), (0, 8 - chunks - 1), (0, 0)))
    first = spectra[0, 0].reshape(n, bw, 2, F)[::stride, :SB].reshape(SRC, 2, F)
    src = whiten(first.astype(jnp.float32)) * keep[::stride, :SB].reshape(SRC, 1, 1).astype(jnp.float32)
    src = src.astype(jnp.bfloat16).transpose(1, 0, 2).reshape(2 * SRC, F)
    cross = exchange(x, aux, src, n, bw, capp)
    return to_lags(cross, table, bw)


def solution(mesh):
    placed = (P("tm", "chan", None, None, None), P("tm", "chan", None))
    return jax.shard_map(
        functools.partial(local, lag_table()),
        mesh=mesh, in_specs=placed, out_specs=P("tm", "chan", None), check_vma=False,
    )
```

time: 1050 us -> 380 us (0.36)
  waiting for transfers between devices: 389 us -> 0 us
  Pallas kernels: 0 us -> 357 us
  local copies, waits for them, and re-layouts: 266 us -> 17.4 us
  matrix products: 216 us -> 0.19 us
  other arithmetic: 111 us -> 4.39 us
  blocking collectives: 36.9 us -> 0 us
  starting transfers between devices: 15 us -> 0 us
  between operations: 14.2 us -> 0.05 us
    pallas_call x0 -> x2, Pallas kernels: none -> 357 us  [the longest x1 321 us: exchange(): pl.pallas_call(functools.partial(exchange_kernel, n, bw, capp), out_shape...]
    all_to_all x2 -> x0, waiting for transfers between devices: 354 us -> none  [the longest x1 351 us: local(): lax.all_to_all(by_owner, 'chan', split_axis=1, concat_axis=0, tiled=True)]
    dot_general x3 -> x1, matrix products: 216 us -> 0.19 us  [local(): jnp.dot(keep.astype(jnp.bfloat16), upto.astype(jnp.bfloat16), preferred_e...]
    squeeze x1 -> x0, local copies, waits for them, and re-layouts: 100 us -> none  [local(): received = got_rows[:, 0]]
    all_to_all x1 -> x0, local copies, waits for them, and re-layouts: 100 us -> none  [local(): lax.all_to_all(by_owner, 'chan', split_axis=1, concat_axis=0, tiled=True)]
    div x1 -> x0, local copies, waits for them, and re-layouts: 54.9 us -> none  [local(): return lagged / jnp.maximum(count_part, 1.0)[:, :, None]]
    reduce_scatter x1 -> x0, waiting for transfers between devices: 31.8 us -> none  [local(): lax.psum_scatter(lagged_all, 'tm', scatter_dimension=0, tiled=True)]
    convert_element_type x4 -> x2, other arithmetic: 31.2 us -> 0.73 us  [the longest x1 0.72 us: local(): first.astype(jnp.float32)]
  transfers between devices with their start and end apart: 4 -> 0, of which waited for: 4 -> 0; matrix products, arithmetic and copies ran while one was open for 12% -> 0% of each run, Pallas kernels for 0% -> 0%
where the time goes in v1:
time: 380 us; the launch traced here: 379 us
  Pallas kernels  357 us (94%)
  local copies, waits for them, and re-layouts  17.4 us (5%)
  other arithmetic  4.39 us (1%)
    pallas_call x1, Pallas kernels, exchange(): pl.pallas_call(functools.partial(exchange_kernel, n, bw, capp), out_shape...  321 us
    pallas_call x1, Pallas kernels, to_lags(): pl.pallas_call(functools.partial(lags_kernel, bw), grid=(-(-LAGS // TILE)...  36.1 us
    unnamed x4, local copies, waits for them, and re-layouts  17.1 us

profile of v1, /device:TPU:15, one launch (start us, length us, event | category | flops | bytes accessed | tf_op | source)
XLA Modules:
  0.0 379.1 jit_solution(10090962864025754926)
XLA Ops:
  0.0 0.8 multiply_reduce_fusion
  0.8 0.1 rsqrt.12
  0.9 0.7 slice_convert_fusion
  1.6 0.5 broadcast.50
  2.2 1.5 reduce.4
  3.7 0.2 fusion.3
  3.9 0.1 convert_element_type.49
  4.0 0.7 fusion.7.src_ref
  4.7 0.1 convert_element_type.45
  4.8 0.6 select_maximum_fusion.aux_ref
  5.4 14.5 %copy.17 = bf16[1,1,10240,2,384]{4,2,3,1,0:T(8,128)(2,1)} copy(bf16[1,1,10240,2,384]{4,3,2,1,0:T(2,128)(2,1)} %param.3) | data formatting | bytes 31457280 | tf_op args[0]
  19.9 320.9 %exchange_correlate.1.cross_ref = bf16[4,640,768]{2,1,0:T(8,128)(2,1)} custom-call(bf16[2,10240,384]{2,1,0:T(8,128)(2,1)} %bitcast.18, f32[16,8,128]{2,1,0:T(8,128)} %select_maximum_fusion.aux_ref, bf16[16,384]{1,0:T(8,128)(2,1)} %fusion.7.src_ref), custom_call_target="tpu_custom_call" | custom-call | tf_op jit(solution)/shard_map/exchange_correlate/pallas_call | solution.py:204
  340.9 0.0 copy-start
  340.9 2.1 copy-done
  343.0 36.1 %to_lags.1 = f32[3001,4,640]{2,1,0:T(4,128)} custom-call(bf16[3001,768]{1,0:T(8,128)(2,1)} %constant.17.clone.table_ref, bf16[4,640,768]{2,1,0:T(8,128)(2,1)S(1)} %copy-done), custom_call_target="tpu_custom_call" | custom-call | tf_op jit(solution)/shard_map/to_lags/pallas_call | solution.py:242
  (7 shorter events, 0.1 us)
Async XLA Ops:
  340.9 2.1 copy-start

commit v2 on v1

--- a/solution.py
+++ b/solution.py
@@ -19,7 +19,8 @@
 SRC = SB * STEPS
 LAGS = 3001
 LANES = 128
-TILE = 128
+AHEAD = 6
+TILE = 512
 MESH = pl.DeviceIdType.MESH
 
 
@@ -36,8 +37,13 @@
     return values * lax.rsqrt(energy + 1e-06)
 
 
-def offset(step, n):
-    return n // 2 + (1 - 2 * (step % 2)) * ((step + 1) // 2)
+def partner(me, step, n):
+    k = step % 2 * ((step + 1) // 2 % (n // 2)) + (1 - step % 2) * (n // 2 + step // 2)
+    place, bit = 0, 1
+    while bit < n:
+        place += (me // bit + k // bit) % 2 * bit
+        bit *= 2
+    return place
 
 
 def exchange_kernel(
@@ -62,7 +68,7 @@
     pl.semaphore_wait(barrier, n)
 
     def dest(step):
-        return (me + offset(step, n)) % n
+        return partner(me, step, n)
 
     def load(step):
         rows = pl.ds(pl.multiple_of(dest(step) * bw, bw), bw)
@@ -126,8 +132,14 @@
             copy.start()
         return 0
 
-    lax.fori_loop(0, n - 1, send, 0)
+    def prepare(step, _):
+        load(step + 1).start()
+        pack(step)
+        return 0
+
     last = n - 1
+    lax.fori_loop(0, AHEAD, send, 0)
+    lax.fori_loop(AHEAD, last, prepare, 0)
     pack(last)
     for copy in forward(last, pk.at[last], aux_ref.at[me]):
         copy.start()
@@ -163,18 +175,23 @@
             copy.wait_recv()
         correlate(fw.at[step], aux_fw.at[step])
 
-    wait_forward(last)
-
     def receive(step, _):
         for copy in main(step):
             copy.wait_recv()
         for copy in forward(step, rv.at[step], aux_rv.at[step]):
             copy.start()
+
+        @pl.when(step + AHEAD < last)
+        def _():
+            for copy in main(step + AHEAD):
+                copy.start()
+
         correlate(rv.at[step], aux_rv.at[step])
-        wait_forward(step)
-        return 0
-
-    lax.fori_loop(0, n - 1, receive, 0)
+        wait_forward((step + last) % n)
+        return 0
+
+    lax.fori_loop(0, last, receive, 0)
+    wait_forward(last - 1)
 
     lane = lax.broadcasted_iota(jnp.int32, (1, LANES), 1)
     for q in range(SB):

time: 380 us -> 326 us (0.86)
  Pallas kernels: 357 us -> 302 us
    pallas_call x1, Pallas kernels: 321 us -> 277 us  [exchange(): pl.pallas_call(functools.partial(exchange_kernel, n, bw, capp), out_shape...]
    pallas_call x1, Pallas kernels: 36.1 us -> 24.3 us  [to_lags(): pl.pallas_call(functools.partial(lags_kernel, bw), grid=(-(-LAGS // TILE)...]
where the time goes in v2:
time: 326 us; the launch traced here: 324 us
  Pallas kernels  302 us (93%)
  local copies, waits for them, and re-layouts  17.4 us (5%)
  other arithmetic  4.39 us (1%)
    pallas_call x1, Pallas kernels, exchange(): pl.pallas_call(functools.partial(exchange_kernel, n, bw, capp), out_shape...  277 us
    pallas_call x1, Pallas kernels, to_lags(): pl.pallas_call(functools.partial(lags_kernel, bw), grid=(-(-LAGS // TILE)...  24.3 us
    unnamed x4, local copies, waits for them, and re-layouts  17.1 us

profile of v2, /device:TPU:15, one launch (start us, length us, event | category | flops | bytes accessed | tf_op | source)
XLA Modules:
  0.0 323.6 jit_solution(16097840327244620028)
XLA Ops:
  0.0 0.8 multiply_reduce_fusion
  0.8 0.1 rsqrt.12
  0.9 0.7 slice_convert_fusion
  1.6 0.5 broadcast.50
  2.2 1.5 reduce.4
  3.7 0.2 fusion.3
  3.9 0.1 convert_element_type.49
  4.0 0.7 fusion.7.src_ref
  4.7 0.1 convert_element_type.45
  4.8 0.6 select_maximum_fusion.aux_ref
  5.4 14.5 %copy.17 = bf16[1,1,10240,2,384]{4,2,3,1,0:T(8,128)(2,1)} copy(bf16[1,1,10240,2,384]{4,3,2,1,0:T(2,128)(2,1)} %param.3) | data formatting | bytes 31457280 | tf_op args[0]
  19.9 277.2 %exchange_correlate.1.cross_ref = bf16[4,640,768]{2,1,0:T(8,128)(2,1)} custom-call(bf16[2,10240,384]{2,1,0:T(8,128)(2,1)} %bitcast.18, f32[16,8,128]{2,1,0:T(8,128)} %select_maximum_fusion.aux_ref, bf16[16,384]{1,0:T(8,128)(2,1)} %fusion.7.src_ref), custom_call_target="tpu_custom_call" | custom-call | tf_op jit(solution)/shard_map/exchange_correlate/pallas_call | solution.py:221
  297.2 0.0 copy-start
  297.2 2.1 copy-done
  299.3 24.3 %to_lags.1 = f32[3001,4,640]{2,1,0:T(4,128)} custom-call(bf16[3001,768]{1,0:T(8,128)(2,1)} %constant.17.clone.table_ref, bf16[4,640,768]{2,1,0:T(8,128)(2,1)S(1)} %copy-done), custom_call_target="tpu_custom_call" | custom-call | tf_op jit(solution)/shard_map/to_lags/pallas_call | solution.py:259
  (7 shorter events, 0.1 us)
Async XLA Ops:
  297.2 2.1 copy-start
